TPU v7x, 256 devices: a whole 4x4x8 slice. The times are simulated.
256 devices in a mesh: dp: 16 (over z_hi, x, core), worker: 16 (over y, z_lo).
Axes of the slice: x: 4, y: 4, z: 8 (z_hi: 2, z_lo: 4; z = z_hi * 4 + z_lo), core: 2. Of those that a mesh axis runs over, the one named last changes fastest.
Arguments:
- activations: bfloat16 [3072, 4096], P('dp', 'worker'), may hold values from -12 to 12
- out_grads: bfloat16 [3072, 4096], P('dp', 'worker'), may hold values from -0.21875 to 0.21875
- old_input: float32 [4096, 4096], P('dp', 'worker'), may hold values from -1.5 to 1.5
- old_output: float32 [4096, 4096], P('dp', 'worker'), may hold values from -1.5 to 1.5
- input_basis: bfloat16 [4096, 4096], P('dp', 'worker'), may hold values from -0.09375 to 0.09375
- output_basis: bfloat16 [4096, 4096], P('worker', 'dp'), may hold values from -0.09375 to 0.09375
- input_eigen: float32 [4096], P('dp'), may hold values from 0.5 to 2
- output_eigen: float32 [4096], P('worker'), may hold values from 0.5 to 2
Outputs:
- input_factor: float32 [4096, 4096], P('dp', 'worker')
- output_factor: float32 [4096, 4096], P('dp', 'worker')
- preconditioned: float32 [4096, 4096], P('dp', 'worker')
All inputs are finite; a program needn't handle non-finite values.
Results may differ from a plain program's by a relative error of at most 0.0059.
Values may be sent and summed in bfloat16 or wider, within the bound.
A program may use at most 64 MiB of HBM per device.

v0:
```python
import jax
import jax.numpy as jnp
from jax import lax
from jax.experimental import pallas as pl
from jax.experimental.pallas import tpu as pltpu
from jax.sharding import PartitionSpec as P

decay_rate = 0.8
damping = 0.1
BF = jnp.bfloat16
F32 = jnp.float32
MESH = pl.DeviceIdType.MESH
N = 16
contract_first = (((0,), (0,)), ((), ()))
contract_last = (((1,), (1,)), ((), ()))

A_ROW, G_COL, U_ROW, V_ROW, G_ROW, A_COL, BACK, BACK2 = range(8)


def dot(a, b, dims=(((1,), (0,)), ((), ()))):
    return lax.dot_general(a, b, dims, preferred_element_type=F32)


def kernel(
    a_ref, g_ref, old_in_ref, old_out_ref, u_ref, v_ref, e_in_ref, e_out_ref,
    in_factor_ref, out_factor_ref, p_ref,
    a_row, g_col, u_row, v_row, g_row, a_col, sc, bk, old,
    u_sib, m_own, w_f32, w_part, w_t, w_y, w_z, w_zsend, wt_own, wt_sib, r_part, r_x, r_z, r_zsend, r_f32,
    e_opp, e_own, acc, p_acc, scale,
    ls, gs, gr, ps, pr, xs, xr,
):
    total_tokens = a_ref.shape[0] * N
    d = lax.axis_index("dp")
    w = lax.axis_index("worker")
    zh, x, c = d // 8, (d // 2) % 4, d % 2
    y, zl = w // 4, w % 4

    def dp_at(r):
        return ((zh + r[0]) % 2 * 4 + (x + r[1]) % 4) * 2 + (c + r[2]) % 2

    def wk_at(r):
        return (y + r[0]) % 4 * 4 + (zl + r[1]) % 4

    def dp_dev(r):
        return (dp_at(r), w)

    def wk_dev(r):
        return (d, wk_at(r))

    partner = (w, d)
    off_diagonal = d != w
    SIB, OPP = (0, 0, 1), (1, 0, 0)

    local = [
        pltpu.make_async_copy(src, dst, ls.at[i])
        for i, (src, dst) in enumerate((
            (a_ref, a_col.at[d]), (u_ref, u_row.at[w]), (g_ref, g_col.at[d]), (v_ref, v_row.at[d]),
            (old_in_ref, old.at[0]), (old_out_ref, old.at[1]),
        ))
    ]
    for copy in local:
        copy.start()

    barrier = pltpu.get_barrier_semaphore()
    peers = [dp_dev(SIB), dp_dev(OPP)]
    for j in (1, 2, 3):
        peers += [dp_dev((0, j, 0)), wk_dev((j, 0)), wk_dev((0, j))]
    for peer in peers:
        pl.semaphore_signal(barrier, inc=1, device_id=peer, device_id_type=MESH)

    @pl.when(off_diagonal)
    def _():
        pl.semaphore_signal(barrier, inc=1, device_id=partner, device_id_type=MESH)

    pl.semaphore_wait(barrier, len(peers) + off_diagonal.astype(jnp.int32))

    sent = []
    pending = {}

    def send(src, dst, ssem, rsem, device, cond=None):
        copy = pltpu.make_async_remote_copy(
            src_ref=src, dst_ref=dst, send_sem=ssem, recv_sem=rsem,
            device_id=device, device_id_type=MESH,
        )
        if cond is None:
            copy.start()
        else:
            pl.when(cond)(copy.start)
        sent.append((copy, cond))

    def arrived(key):
        dst, rsem = pending.pop(key)
        pltpu.make_async_remote_copy(
            src_ref=dst, dst_ref=dst, send_sem=rsem, recv_sem=rsem,
            device_id=dp_dev(SIB), device_id_type=MESH,
        ).wait_recv()

    def message(key, src, dst, device, lands=None):
        i = len(messages)
        messages.append(key)
        send(src, dst, xs.at[i], xr.at[i], device)
        pending[key] = (dst if lands is None else lands, xr.at[i])

    messages = []
    counts = [0] * 8
    unsent = {}
    chained = {}
    bufs = [a_row, g_col, u_row, v_row, g_row, a_col, bk.at[0], bk.at[1]]

    def push(op, slot, to):
        mirror = tuple((a - b) % n for a, b, n in zip(slot, to, (2, 4, 2)))
        i = (mirror[0] * 4 + mirror[1]) * 2 + mirror[2]
        view = bufs[op].at[dp_at(slot)]
        send(view, view, gs.at[op, counts[op]], gr.at[op, i], dp_dev(to))
        counts[op] += 1
        pending[op, mirror] = (bufs[op].at[dp_at(mirror)], gr.at[op, i])

    def got(op, slot):
        arrived((op, slot))

    def dp_start(op):
        push(op, (0, 0, 0), OPP)
        for j in (2, 1, 3):
            push(op, (0, 0, 0), (0, j, 0))
        push(op, (0, 0, 0), SIB)

    def dp_opposite(op):
        got(op, OPP)
        for j in (2, 1, 3):
            push(op, OPP, (0, j, 0))
        push(op, OPP, SIB)

    def dp_share(op):
        for z in (0, 1):
            for j in (1, 3, 2):
                got(op, (z, j, 0))
                push(op, (z, j, 0), SIB)

    def dp_finish(op):
        for z in (0, 1):
            for j in (0, 1, 3, 2):
                got(op, (z, j, 1))

    upper = zl >= 2
    middle = jnp.logical_or(zl == 1, zl == 2)

    def line(v):
        return jnp.where(upper, 3 - v, v)

    inner = line(jnp.where(middle, 2, 1))
    outer = line(0)
    z_order = (zl, line(jnp.where(middle, 0, 1)), line(2), line(3))

    def wk_slot(op, iy, n):
        return bufs[op].at[(y + iy) % 4 * 4 + z_order[n]]

    def wk_send(op, src, dst, i, device, cond=None):
        send(src, dst, gs.at[op, counts[op]], gr.at[op, i], device, cond)
        counts[op] += 1

    def wk_line(op, n, to, cond):
        view = wk_slot(op, 0, n)
        wk_send(op, view, view, 16 + z_order[n], (d, y * 4 + to), cond)

    def wk_both(op, n):
        for iy in (1, 3):
            view = wk_slot(op, 0, n)
            i = (4 - iy) * 4 + n
            wk_send(op, view, view, i, wk_dev((iy, 0)))
            pending[op, 4 - iy, n] = (wk_slot(op, 4 - iy, n), gr.at[op, i])

    def wk_start(op, along_y=True, direct=False):
        if direct:
            for n in (1, 2, 3):
                view = wk_slot(op, 0, 0)
                wk_send(op, view, view, 16 + zl, (d, y * 4 + z_order[n]))
        else:
            wk_line(op, 0, inner, None)
            wk_line(op, 0, outer, middle)
        for n in (1, 2, 3):
            pending[op, 0, n] = (wk_slot(op, 0, n), gr.at[op, 16 + z_order[n]])
        unsent[op] = [1, 2, 3]
        chained[op] = not direct
        if along_y:
            wk_both(op, 0)

    def wk_chain(op, *ns):
        for n in ns:
            arrived((op, 0, n))
            if chained[op]:
                wk_line(op, n, inner if n == 1 else outer, middle)
            unsent[op].remove(n)

    def wk_forward(op, *ns):
        for n in ns:
            wk_chain(op, n)
            wk_both(op, n)

    def wk_cross(op, *ns):
        for n in ns:
            for h, iy in ((0, 3), (1, 1)):
                arrived((op, iy, n))
                size = bufs[op].shape[1] // 2
                rows = pl.ds(h * size, size)
                view = wk_slot(op, iy, n).at[rows]
                i = h * 8 + n
                wk_send(op, view, view, i, wk_dev((4 - iy, 0)))
                pending[op, 2, n, h] = (wk_slot(op, 2, n).at[rows], gr.at[op, i])

    def wk_finish(op, *ns):
        for n in ns:
            for h in (0, 1):
                arrived((op, 2, n, h))

    def turn(i, src, dst):
        return pltpu.make_async_remote_copy(
            src_ref=src.at[d], dst_ref=dst.at[d], send_sem=ps.at[i], recv_sem=pr.at[i],
            device_id=partner, device_id_type=MESH,
        )

    def turn_start(i, src, dst):
        @pl.when(off_diagonal)
        def _():
            turn(i, src, dst).start()

        @pl.when(jnp.logical_not(off_diagonal))
        def _():
            dst[w] = src[d]

    def turn_finish(i, src, dst):
        @pl.when(off_diagonal)
        def _():
            turn(i, src, dst).wait()

    def finish():
        for op in unsent:
            wk_chain(op, *list(unsent[op]))
        for key in list(pending):
            arrived(key)
        for copy, cond in sent:
            if cond is None:
                copy.wait_send()
            else:
                pl.when(cond)(copy.wait_send)

    def gram(left, right, slots=None):
        if slots is None:
            acc[...] = jnp.zeros_like(acc)

        def four(first):
            acc[...] += sum(dot(left[first + t], right[first + t], contract_first) for t in range(4))

        if slots is not None:
            four(slots(0))
        else:
            pl.loop(0, N, step=4)(four)

    local[0].wait()
    turn_start(0, a_col, a_row)
    local[2].wait()
    dp_start(G_COL)
    local[1].wait()
    wk_start(U_ROW)
    for copy in local[3:]:
        copy.wait()
    dp_start(V_ROW)
    e_own[...] = jnp.broadcast_to(e_in_ref[...], e_own.shape)
    message("e", e_own, e_opp, dp_dev(OPP))
    wk_forward(U_ROW, 1)
    wk_cross(U_ROW, 0)
    dp_opposite(G_COL)
    turn_finish(0, a_col, a_row)
    wk_start(A_ROW)
    wk_chain(U_ROW, 2)
    wk_forward(A_ROW, 1)
    wk_cross(A_ROW, 0)
    arrived("e")
    column = jnp.broadcast_to(e_out_ref[...], acc.shape).T
    scale[0] = column * e_opp[0:1, :] + damping
    scale[1] = column * e_own[0:1, :] + damping
    wk_forward(A_ROW, 2)
    wk_chain(U_ROW, 3)
    wk_cross(A_ROW, 1)
    wk_forward(A_ROW, 3)
    turn_start(1, g_col, g_row)
    wk_both(U_ROW, 2)
    wk_cross(A_ROW, 2)
    dp_share(G_COL)
    wk_cross(A_ROW, 3)
    dp_opposite(V_ROW)
    wk_both(U_ROW, 3)
    dp_finish(G_COL)

    acc[...] = jnp.zeros_like(acc)
    for iy in (0, 1, 3):
        gram(a_row, g_col, lambda t, iy=iy: (y + iy) % 4 * 4 + t)
    wk_cross(U_ROW, 1)
    wk_finish(A_ROW, 0, 1, 2, 3)
    gram(a_row, g_col, lambda t: (y + 2) % 4 * 4 + t)
    m_own[...] = acc[...].astype(BF)
    dp_start(A_COL)
    dp_share(V_ROW)
    dp_finish(V_ROW)

    size = m_own.shape[0] // 2
    cols = [pl.ds(q * size, size) for q in (0, 1)]
    order = (2, 1, 3, 0)
    ways = ((0, 1), (1, 3))

    def w_block(iy, iz):
        return dot(m_own[...], v_row[wk_at((iy, iz))])

    def w_transit(q):
        for iz in order:
            for i, to in ways:
                message(("t", q, i, iz), w_part.at[q, 2, iz, cols[i]], w_t.at[q, i, iz], wk_dev((to, 0)))

    def w_along_y(q):
        for iz in order:
            for i, to in ways:
                arrived(("t", q, i, iz))
                w_part[q, to, iz] = w_f32[to, iz, :, cols[q]].astype(BF)
                w_part[q, to, iz, cols[i]] = (
                    w_f32[to, iz, cols[i], cols[q]] + w_t[q, i, iz].astype(F32)
                ).astype(BF)
                message(("y", q, i, iz), w_part.at[q, to, iz], w_y.at[q, i, iz], wk_dev((to, 0)))

    def w_along_z(q):
        for iz in order:
            for i, _ in ways:
                arrived(("y", q, i, iz))
            total = w_f32[0, iz, :, cols[q]] + w_y[q, 0, iz].astype(F32) + w_y[q, 1, iz].astype(F32)
            if iz:
                w_zsend[q, iz] = total.astype(BF)
                message(("z", q, iz), w_zsend.at[q, iz], w_z.at[q, iz], wk_dev((0, iz)))
            else:
                w_f32[0, 0, :, cols[q]] = total

    def w_done(q):
        for iz in (1, 3, 2):
            arrived(("z", q, iz))
        total = w_f32[0, 0, :, cols[q]]
        for iz in (1, 2, 3):
            total += w_z[q, iz].astype(F32)
        wt_own[q] = total.T.astype(BF)
        message(("w", q), wt_own.at[q], wt_sib.at[q], dp_dev(SIB))

    def r_block(q, h, j):
        k = (zh + 1 - h) % 2 * 4 + (x + j) % 4
        return dot(wt_own[q], u_row[2 * k + c]) + dot(wt_sib[q], u_sib[k])

    def r_along_x(q):
        arrived(("w", q))
        for j in (2, 1, 3):
            for h in (0, 1):
                r_part[q, j, h] = r_block(q, h, j).astype(BF)
            message(("r", q, j), r_part.at[q, j], r_x.at[q, j], dp_dev((0, j, 0)))
        for h in (0, 1):
            r_f32[q, h] = r_block(q, h, 0)

    def r_across(q):
        for j in (1, 3, 2):
            arrived(("r", q, j))
        for h in (0, 1):
            total = r_f32[q, h]
            for j in (1, 2, 3):
                total += r_x[q, j, h].astype(F32)
            r_f32[q, h] = total
            r_zsend[q, 1 - h] = total.astype(BF)
        message(("rz", q), r_zsend.at[q], r_z.at[q], dp_dev(OPP))

    def scaled_start(q):
        arrived(("rz", q))
        for h in (0, 1):
            spectral = r_f32[q, h] + r_z[q, h].astype(F32)
            sc[q, x, c, (zh + 1 - h) % 2] = (spectral / scale[h, cols[q], :]).astype(BF)
        own = sc.at[q, x, c]
        for j in (2, 1, 3):
            there = sc.at[q, (x + 4 - j) % 4, c]
            message(("sx", q, 4 - j), own, own, dp_dev((0, j, 0)), there)
        message(("sc", q, 0), own, own, dp_dev(SIB), sc.at[q, x, 1 - c])

    def scaled_share(q):
        for j in (1, 3, 2):
            arrived(("sx", q, j))
            view = sc.at[q, (x + j) % 4, c]
            message(("sc", q, j), view, view, dp_dev(SIB), sc.at[q, (x + j) % 4, 1 - c])

    def back(q):
        for j in (0, 1, 3, 2):
            arrived(("sc", q, j))
        total = jnp.zeros((2 * size, size), F32)
        for i in range(N):
            total += dot(u_row[i], sc[q, (i // 2) % 4, i % 2, i // 8], contract_last)
        bk[q, w] = total.astype(BF)
        wk_start(BACK + q, direct=True)

    def project(q):
        @pl.loop(0, N, step=4)
        def _(i):
            p_acc[...] += sum(dot(bk[q, i + t], v_row[i + t, :, cols[q]], contract_last) for t in range(4))

    for iz in order:
        block = w_block(2, iz).astype(BF)
        for q in (0, 1):
            w_part[q, 2, iz] = block[:, q * size : (q + 1) * size]
    w_transit(0)
    w_transit(1)
    for iy in (1, 3, 0):
        for iz in order:
            w_f32[iy, iz] = w_block(iy, iz)
    turn_finish(1, g_col, g_row)
    wk_start(G_ROW, along_y=False)
    w_along_y(0)
    wk_cross(U_ROW, 2, 3)
    w_along_y(1)
    wk_both(G_ROW, 0)
    dp_opposite(A_COL)
    w_along_z(0)
    wk_forward(G_ROW, 1)
    wk_finish(U_ROW, 0, 1, 2, 3)
    for k in range(8):
        message(("u", k), u_row.at[2 * k + 1 - c], u_sib.at[k], dp_dev(SIB))
    w_done(0)
    w_along_z(1)
    for k in range(8):
        arrived(("u", k))
    r_along_x(0)
    wk_forward(G_ROW, 2)
    w_done(1)
    wk_cross(G_ROW, 0)
    r_across(0)
    r_along_x(1)
    dp_share(A_COL)
    wk_forward(G_ROW, 3)
    wk_cross(G_ROW, 1)
    scaled_start(0)
    r_across(1)
    dp_finish(A_COL)

    gram(a_row, a_col)
    in_factor_ref[...] = decay_rate * old[0] + ((1.0 - decay_rate) / total_tokens) * acc[...]
    wk_cross(G_ROW, 2)
    scaled_share(0)
    scaled_start(1)
    wk_cross(G_ROW, 3)
    back(0)
    scaled_share(1)
    wk_cross(BACK, 0)
    wk_forward(BACK, 1)
    back(1)
    wk_forward(BACK, 2, 3)
    wk_cross(BACK, 1)
    wk_cross(BACK2, 0)
    wk_finish(G_ROW, 0, 1, 2, 3)
    gram(g_row, g_col)
    out_factor_ref[...] = decay_rate * old[1] + (1.0 - decay_rate) * acc[...]
    wk_cross(BACK, 2, 3)
    wk_forward(BACK2, 1, 2, 3)
    p_acc[...] = jnp.zeros_like(p_acc)
    wk_finish(BACK, 0, 1, 2, 3)
    wk_cross(BACK2, 1, 2)
    project(0)
    wk_cross(BACK2, 3)
    wk_finish(BACK2, 0, 1, 2, 3)
    project(1)
    p_ref[...] = p_acc[...]
    assert not pending
    finish()


def body(activations, out_grads, old_input, old_output, input_basis, output_basis, input_eigen, output_eigen):
    tokens, feats = activations.shape
    block = (feats, feats)
    low, thin, quarter = (feats // 2, feats), (feats, feats // 2), (feats // 2, feats // 2)
    vmem = pl.BlockSpec(memory_space=pltpu.VMEM)
    hbm = pl.BlockSpec(memory_space=pl.ANY)
    dma = pltpu.SemaphoreType.DMA
    out = jax.ShapeDtypeStruct(block, F32)
    return pl.pallas_call(
        kernel,
        out_shape=(out, out, out),
        in_specs=[hbm] * 6 + [vmem] * 2,
        out_specs=(vmem, vmem, vmem),
        scratch_shapes=[
            pltpu.VMEM((N, tokens, feats), BF),
            pltpu.VMEM((N, tokens, feats), BF),
            pltpu.VMEM((N,) + block, BF),
            pltpu.VMEM((N,) + block, BF),
            pltpu.VMEM((N, tokens, feats), BF),
            pltpu.VMEM((N, tokens, feats), BF),
            pltpu.VMEM((2, 4, 2, 2) + low, BF),
            pltpu.VMEM((2, N) + thin, BF),
            pltpu.VMEM((2,) + block, F32),
            pltpu.VMEM((8,) + block, BF),
            pltpu.VMEM(block, BF),
            pltpu.VMEM((4, 4) + block, F32),
            pltpu.VMEM((2, 4, 4) + thin, BF),
            pltpu.VMEM((2, 2, 4) + quarter, BF),
            pltpu.VMEM((2, 2, 4) + thin, BF),
            pltpu.VMEM((2, 4) + thin, BF),
            pltpu.VMEM((2, 4) + thin, BF),
            pltpu.VMEM((2,) + low, BF),
            pltpu.VMEM((2,) + low, BF),
            pltpu.VMEM((2, 4, 2) + low, BF),
            pltpu.VMEM((2, 4, 2) + low, BF),
            pltpu.VMEM((2, 2) + low, BF),
            pltpu.VMEM((2, 2) + low, BF),
            pltpu.VMEM((2, 2) + low, F32),
            pltpu.VMEM((8, feats), F32),
            pltpu.VMEM((8, feats), F32),
            pltpu.VMEM(block, F32),
            pltpu.VMEM(block, F32),
            pltpu.VMEM((2,) + block, F32),
            dma((6,)),
            dma((8, 24)), dma((8, 24)),
            dma((2,)), dma((2,)),
            dma((80,)), dma((80,)),
        ],
        compiler_params=pltpu.CompilerParams(
            collective_id=0, has_side_effects=True, vmem_limit_bytes=60 << 20
        ),
        cost_estimate=pl.CostEstimate(flops=3_400_000_000, bytes_accessed=4 << 20, transcendentals=0),
        name="kfac",
    )(
        activations, out_grads, old_input, old_output, input_basis, output_basis,
        input_eigen[None, :], output_eigen[None, :],
    )


def solution(mesh):
    in_specs = (
        P("dp", "worker"),
        P("dp", "worker"),
        P("dp", "worker"),
        P("dp", "worker"),
        P("dp", "worker"),
        P("worker", "dp"),
        P("dp"),
        P("worker"),
    )
    out_specs = (P("dp", "worker"), P("dp", "worker"), P("dp", "worker"))
    return jax.shard_map(body, mesh=mesh, in_specs=in_specs, out_specs=out_specs, check_vma=False)
```

profile of v0, /device:TPU:1, one launch (start us, length us, event | category | flops | bytes accessed | tf_op | source)
XLA Modules:
  0.0 144.2 jit_solution(10956227693449454262)
XLA Ops:
  0.6 140.0 %kfac.1 = (f32[256,256]{1,0:T(8,128)}, f32[256,256]{1,0:T(8,128)}, f32[256,256]{1,0:T(8,128)}) custom-call(bf16[192,256]{1,0:T(8,128)(2,1)} %a_ref.1, bf16[192,256]{1,0:T(8,128)(2,1)} %g_ref.1, f32[256,256]{1,0:T(8,128)} %old_in_ref.1, f32[256,256]{1,0:T(8,128)} %old_out_ref.1, bf16[256,256]{1,0:T(8,128)(2,1)} %u_ref.1, bf16[256,256]{1,0:T(8,128)(2,1)} %v_ref.1, ...), custom_call_target="tpu_custom_call" | custom-call | flops 3400000000 | bytes 4194304 | tf_op jit(solution)/shard_map/kfac/pallas_call | solution.py:480
  140.7 0.0 copy-start.1
  140.7 1.7 %copy.14 = f32[256,256]{1,0:T(8,128)} copy(f32[256,256]{1,0:T(8,128)} %get-tuple-element.6) | data formatting | bytes 524288
  142.4 0.0 copy-done.1
  142.4 0.0 copy-start
  142.4 0.7 copy.15
  143.1 0.3 copy-done
  143.4 0.7 copy.16
Async XLA Ops:
  140.7 1.7 %copy-start.1 = (f32[256,256]{1,0:T(8,128)S(1)}, f32[256,256]{1,0:T(8,128)}, u32[]{:S(2)}) copy-start(f32[256,256]{1,0:T(8,128)} %get-tuple-element.7) | copy-start | bytes 786436
  142.4 1.0 copy-start
where the time goes:
time: 144 us
  Pallas kernels  140 us (97%)
  local copies, waits for them, and re-layouts  3.46 us (2%)
    pallas_call x1, Pallas kernels, body(): pl.pallas_call(kernel, out_shape=(out, out, out), in_specs=[hbm] * 6 + [v...  140 us
    unnamed x7, local copies, waits for them, and re-layouts  3.46 us

commit v1 on v0

--- a/solution.py
+++ b/solution.py
@@ -396,9 +396,7 @@
         wk_start(BACK + q, direct=True)
 
     def project(q):
-        @pl.loop(0, N, step=4)
-        def _(i):
-            p_acc[...] += sum(dot(bk[q, i + t], v_row[i + t, :, cols[q]], contract_last) for t in range(4))
+        p_acc[...] += sum(dot(bk[q, i], v_row[i, :, cols[q]], contract_last) for i in range(N))
 
     for iz in order:
         block = w_block(2, iz).astype(BF)

time: 144 us -> 144 us (level)
  no operation moved by 1% of the time
where the time goes in v1:
time: 144 us
  Pallas kernels  140 us (97%)
  local copies, waits for them, and re-layouts  3.46 us (2%)
    pallas_call x1, Pallas kernels, body(): pl.pallas_call(kernel, out_shape=(out, out, out), in_specs=[hbm] * 6 + [v...  140 us
    unnamed x7, local copies, waits for them, and re-layouts  3.46 us

profile of v1, /device:TPU:1, one launch (start us, length us, event | category | flops | bytes accessed | tf_op | source)
XLA Modules:
  0.0 144.2 jit_solution(16408774960070680449)
XLA Ops:
  0.6 140.1 %kfac.1 = (f32[256,256]{1,0:T(8,128)}, f32[256,256]{1,0:T(8,128)}, f32[256,256]{1,0:T(8,128)}) custom-call(bf16[192,256]{1,0:T(8,128)(2,1)} %a_ref.1, bf16[192,256]{1,0:T(8,128)(2,1)} %g_ref.1, f32[256,256]{1,0:T(8,128)} %old_in_ref.1, f32[256,256]{1,0:T(8,128)} %old_out_ref.1, bf16[256,256]{1,0:T(8,128)(2,1)} %u_ref.1, bf16[256,256]{1,0:T(8,128)(2,1)} %v_ref.1, ...), custom_call_target="tpu_custom_call" | custom-call | flops 3400000000 | bytes 4194304 | tf_op jit(solution)/shard_map/kfac/pallas_call | solution.py:478
  140.7 0.0 copy-start.1
  140.7 1.7 %copy.14 = f32[256,256]{1,0:T(8,128)} copy(f32[256,256]{1,0:T(8,128)} %get-tuple-element.6) | data formatting | bytes 524288
  142.4 0.0 copy-done.1
  142.4 0.0 copy-start
  142.5 0.7 copy.15
  143.2 0.3 copy-done
  143.5 0.7 copy.16
Async XLA Ops:
  140.7 1.7 %copy-start.1 = (f32[256,256]{1,0:T(8,128)S(1)}, f32[256,256]{1,0:T(8,128)}, u32[]{:S(2)}) copy-start(f32[256,256]{1,0:T(8,128)} %get-tuple-element.7) | copy-start | bytes 786436
  142.4 1.0 copy-start
